TPU v7x, 256 devices: a whole 4x4x8 slice. The times are simulated.
256 devices in a mesh: row: 8 (over y_hi, x), col: 32 (over z, y_lo, core).
Axes of the slice: x: 4, y: 4 (y_hi: 2, y_lo: 2; y = y_hi * 2 + y_lo), z: 8, core: 2. Of those that a mesh axis runs over, the one named last changes fastest.
Arguments:
- tokens: bfloat16 [1280, 7168], P('col', 'row'), may hold values from -6 to 6
- cotangent: bfloat16 [1280, 7168], P('col', 'row'), may hold values from -6 to 6
- w_gate: bfloat16 [7168, 16384], P('row', 'col'), may hold values from -0.0625 to 0.0625
- w_up: bfloat16 [7168, 16384], P('row', 'col'), may hold values from -0.0625 to 0.0625
- w_down: bfloat16 [16384, 7168], P('col', 'row'), may hold values from -0.046875 to 0.046875
Outputs:
- grad_tokens: bfloat16 [1280, 7168], P('col', 'row')
- grad_w_gate: bfloat16 [7168, 16384], P('row', 'col')
- grad_w_up: bfloat16 [7168, 16384], P('row', 'col')
- grad_w_down: bfloat16 [16384, 7168], P('col', 'row')
All inputs are finite; a program needn't handle non-finite values.
Results may differ from a plain program's by a relative error of at most 0.0049.
Values may be sent and summed in bfloat16 or wider, within the bound.
A program may use at most 64 MiB of HBM per device.

v0:
```python
import jax
import jax.numpy as jnp
from jax import lax
from jax.sharding import PartitionSpec as P


def activate(sums, width):
    gate = sums[:, :width]
    up = sums[:, width : 2 * width]
    back = sums[:, 2 * width :]
    sigma = jax.nn.sigmoid(gate)
    silu = gate * sigma
    hidden = (silu * up).astype(jnp.bfloat16)
    grad_gate = (back * up * sigma * (1.0 + gate * (1.0 - sigma))).astype(jnp.bfloat16)
    grad_up = (back * silu).astype(jnp.bfloat16)
    return (hidden, grad_gate, grad_up)


def local(tokens, cotangent, w_gate, w_up, w_down):
    token_all, cotan_all = (
        lax.all_gather(tokens, "col", axis=0, tiled=True),
        lax.all_gather(cotangent, "col", axis=0, tiled=True),
    )
    width = w_gate.shape[1]
    last_last = (((1,), (1,)), ((), ()))
    first_first = (((0,), (0,)), ((), ()))
    gate = jnp.dot(token_all, w_gate, preferred_element_type=jnp.float32)
    up = jnp.dot(token_all, w_up, preferred_element_type=jnp.float32)
    back = lax.dot_general(cotan_all, w_down, last_last, preferred_element_type=jnp.float32)
    sums = lax.psum_scatter(
        jnp.concatenate([gate, up, back], axis=1), "row", scatter_dimension=0, tiled=True
    )
    own_hidden, own_gate, own_up = activate(sums, width)
    hidden, grad_gate, grad_up = (
        lax.all_gather(own_hidden, "row", axis=0, tiled=True),
        lax.all_gather(own_gate, "row", axis=0, tiled=True),
        lax.all_gather(own_up, "row", axis=0, tiled=True),
    )
    total = lax.dot_general(grad_gate, w_gate, last_last, preferred_element_type=jnp.float32)
    grad_tokens = lax.psum_scatter(
        total + lax.dot_general(grad_up, w_up, last_last, preferred_element_type=jnp.float32),
        "col",
        scatter_dimension=0,
        tiled=True,
    ).astype(jnp.bfloat16)
    grad_w_down = lax.dot_general(
        hidden, cotan_all, first_first, preferred_element_type=jnp.float32
    ).astype(jnp.bfloat16)
    grad_w_gate = lax.dot_general(
        token_all, grad_gate, first_first, preferred_element_type=jnp.float32
    ).astype(jnp.bfloat16)
    grad_w_up = lax.dot_general(
        token_all, grad_up, first_first, preferred_element_type=jnp.float32
    ).astype(jnp.bfloat16)
    return (grad_tokens, grad_w_gate, grad_w_up, grad_w_down)


def solution(mesh):
    return jax.shard_map(
        local,
        mesh=mesh,
        in_specs=(
            P("col", "row"),
            P("col", "row"),
            P("row", "col"),
            P("row", "col"),
            P("col", "row"),
        ),
        out_specs=(P("col", "row"), P("row", "col"), P("row", "col"), P("col", "row")),
        check_vma=False,
    )
```

profile of v0, /device:TPU:1, one launch (start us, length us, event | category | flops | bytes accessed | tf_op | source)
XLA Modules:
  0.0 578.6 jit_solution(11193675631867982537)
XLA Ops:
  7.2 0.0 copy-start
  7.2 0.0 all-gather.6.cloned.1.call-start
  7.2 0.7 all-gather.6.cloned.1.call-update
  7.9 0.0 all-gather.8.cloned.1.call-start
  8.0 0.7 all-gather.8.cloned.1.call-update
  8.7 0.0 reduce-scatter.8.cloned.1.call-start
  8.7 70.6 %all-gather.6.cloned.1.call-done = bf16[1280,896]{1,0:T(8,128)(2,1)} async-done(((bf16[40,896]{1,0:T(8,128)(2,1)}), bf16[1280,896]{1,0:T(8,128)(2,1)}) %all-gather.6.cloned.1.call-update) | async-done | bytes 2293776 | tf_op jit(solution)/shard_map/all_gather | solution.py:21
  79.3 0.0 copy-start.1
  79.3 5.1 fusion.4
  84.4 0.0 copy-done
  84.4 0.0 copy-done.1
  84.4 3.1 fusion.3
  87.5 58.6 %all-gather.8.cloned.1.call-done = bf16[1280,896]{1,0:T(8,128)(2,1)} async-done(((bf16[40,896]{1,0:T(8,128)(2,1)}), bf16[1280,896]{1,0:T(8,128)(2,1)}) %all-gather.8.cloned.1.call-update) | async-done | bytes 2293776 | tf_op jit(solution)/shard_map/all_gather | solution.py:22
  146.1 0.0 copy-start.2
  146.1 0.0 copy-start.3
  146.1 3.6 fusion.5
  149.7 0.0 copy-done.2
  149.7 0.0 copy-done.3
  149.7 3.4 pad_maximum_fusion
  153.1 9.1 %copy.21 = f32[1280,1536]{1,0:T(8,128)} copy(f32[1280,1536]{0,1:T(8,128)} %pad_maximum_fusion) | data formatting | bytes 15728640
  162.2 0.0 reduce-scatter.8.cloned.1.call-update
  162.2 0.0 all-gather.10.cloned.1.call-start
  162.2 116.9 %reduce-scatter.8.cloned.1.call-done = f32[160,1536]{1,0:T(8,128)} async-done(((f32[1280,1536]{1,0:T(8,128)}), f32[160,1536]{1,0:T(8,128)}) %reduce-scatter.8.cloned.1.call-update) | async-done | bytes 983056 | tf_op jit(solution)/shard_map/reduce_scatter | solution.py:30
  279.1 2.1 multiply_convert_fusion
  281.2 0.0 all-gather.10.cloned.1.call-update
  281.2 0.0 all-gather.12.cloned.1.call-start
  281.3 0.5 all-gather.12.cloned.1.call-update
  281.8 0.0 all-gather.14.cloned.1.call-start
  281.9 0.5 all-gather.14.cloned.1.call-update
  282.4 0.0 reduce-scatter.10.cloned.1.call-start
  282.5 51.6 %all-gather.10.cloned.1.call-done = bf16[1280,512]{1,0:T(8,128)(2,1)} async-done(((bf16[160,512]{1,0:T(8,128)(2,1)}), bf16[1280,512]{1,0:T(8,128)(2,1)}) %all-gather.10.cloned.1.call-update) | async-done | bytes 1310736 | tf_op jit(solution)/shard_map/all_gather | solution.py:36
  334.1 5.0 fusion.6
  339.1 51.7 %all-gather.12.cloned.1.call-done = bf16[1280,512]{1,0:T(8,128)(2,1)} async-done(((bf16[160,512]{1,0:T(8,128)(2,1)}), bf16[1280,512]{1,0:T(8,128)(2,1)}) %all-gather.12.cloned.1.call-update) | async-done | bytes 1310736 | tf_op jit(solution)/shard_map/all_gather | solution.py:37
  390.8 6.6 %convolution_add_fusion = f32[1280,896]{1,0:T(8,128)} fusion(f32[1280,896]{1,0:T(8,128)} %fusion.6, bf16[1280,512]{1,0:T(8,128)(2,1)} %all-gather.12.cloned.1.call-done, bf16[896,512]{1,0:T(8,128)(2,1)} %param.8), kind=kOutput, calls=%fused_computation.1 | convolution fusion | flops 1175552000 | bytes 11403264 | tf_op jit(solution)/shard_map/dot_general | solution.py:41
  397.4 0.0 reduce-scatter.10.cloned.1.call-update
  397.5 3.8 fusion.1
  401.2 2.2 copy.20
  403.5 3.8 fusion
  407.2 2.2 copy.19
  409.4 37.5 %all-gather.14.cloned.1.call-done = bf16[1280,512]{1,0:T(8,128)(2,1)} async-done(((bf16[160,512]{1,0:T(8,128)(2,1)}), bf16[1280,512]{1,0:T(8,128)(2,1)}) %all-gather.14.cloned.1.call-update) | async-done | bytes 1310736 | tf_op jit(solution)/shard_map/all_gather | solution.py:35
  446.9 4.5 convolution_convert_fusion
  451.4 118.8 %reduce-scatter.10.cloned.1.call-done = f32[40,896]{1,0:T(8,128)} async-done(((f32[1280,896]{1,0:T(8,128)}), f32[40,896]{1,0:T(8,128)}) %reduce-scatter.10.cloned.1.call-update) | async-done | bytes 143376
  570.2 1.5 convert_element_type.29
Async XLA Ops:
  7.2 77.2 %copy-start = (bf16[896,512]{1,0:T(8,128)(2,1)S(1)}, bf16[896,512]{1,0:T(8,128)(2,1)}, u32[]{:S(2)}) copy-start(bf16[896,512]{1,0:T(8,128)(2,1)} %param.7) | copy-start | bytes 2752516
  7.2 72.1 %all-gather.6.cloned.1.call-start = ((), (), s32[]{:S(2)}) async-start(), calls=%async_computation.2 | async-start | bytes 2365440 | tf_op jit(solution)/shard_map/all_gather | solution.py:21
  7.9 138.2 %all-gather.8.cloned.1.call-start = ((), (), s32[]{:S(2)}) async-start(), calls=%async_computation.3 | async-start | bytes 2365440 | tf_op jit(solution)/shard_map/all_gather | solution.py:22
  8.7 270.4 %reduce-scatter.8.cloned.1.call-start = ((), (), s32[]{:S(2)}) async-start(), calls=%async_computation.7 | async-start | bytes 8847360 | tf_op jit(solution)/shard_map/reduce_scatter | solution.py:30
  79.3 5.1 copy-start.1
  146.1 3.6 copy-start.2
  146.1 3.6 copy-start.3
  162.2 171.9 %all-gather.10.cloned.1.call-start = ((), (), s32[]{:S(2)}) async-start(), calls=%async_computation.4 | async-start | bytes 1474560 | tf_op jit(solution)/shard_map/all_gather | solution.py:36
  281.2 109.6 %all-gather.12.cloned.1.call-start = ((), (), s32[]{:S(2)}) async-start(), calls=%async_computation.5 | async-start | bytes 1474560 | tf_op jit(solution)/shard_map/all_gather | solution.py:37
  281.8 165.1 %all-gather.14.cloned.1.call-start = ((), (), s32[]{:S(2)}) async-start(), calls=%async_computation.6 | async-start | bytes 1474560 | tf_op jit(solution)/shard_map/all_gather | solution.py:35
  282.4 287.8 %reduce-scatter.10.cloned.1.call-start = ((), (), s32[]{:S(2)}) async-start(), calls=%async_computation.8 | async-start | bytes 4730880
Sparse Core Ops, SparseCore 0:
  9.9 69.3 all-gather.5
  81.1 64.9 all-gather.7
  162.3 116.7 reduce-scatter.7
  282.5 51.5 all-gather.9
  337.5 53.2 all-gather.11
  393.6 53.2 all-gather.13
  449.6 120.5 reduce-scatter.9
where the time goes:
time: 582 us; the launch traced here: 579 us
  waiting for transfers between devices  508 us (87%)
  matrix products  35.4 us (6%)
  between operations  14.2 us (2%)
  local copies, waits for them, and re-layouts  13.5 us (2%)
  other arithmetic  7.05 us (1%)
    unnamed x8, waiting for transfers between devices  121 us
    reduce_scatter x1, waiting for transfers between devices, local(): lax.psum_scatter(jnp.concatenate([gate, up, back], axis=1), 'row', scatte...  117 us
    all_gather x1, waiting for transfers between devices, local(): lax.all_gather(tokens, 'col', axis=0, tiled=True)  70.6 us
    all_gather x1, waiting for transfers between devices, local(): lax.all_gather(cotangent, 'col', axis=0, tiled=True)  58.6 us
    all_gather x1, waiting for transfers between devices, local(): lax.all_gather(own_up, 'row', axis=0, tiled=True)  51.7 us
    all_gather x1, waiting for transfers between devices, local(): lax.all_gather(own_gate, 'row', axis=0, tiled=True)  51.6 us
    all_gather x1, waiting for transfers between devices, local(): lax.all_gather(own_hidden, 'row', axis=0, tiled=True)  37.5 us
    unnamed x11, local copies, waits for them, and re-layouts  13.5 us
  transfers between devices with their start and end apart: 7, of which 7 were waited for; matrix products, arithmetic and copies ran while one was open for 6% of the time, Pallas kernels for 0%

commit v1 on v0

v1 whole, which is shorter than its diff:
```python
import jax
import jax.numpy as jnp
from jax import lax
from jax.experimental import pallas as pl
from jax.experimental.pallas import tpu as pltpu
from jax.sharding import PartitionSpec as P

MESH = pl.DeviceIdType.MESH
BF = jnp.bfloat16
F32 = jnp.float32
LL = (((1,), (1,)), ((), ()))
FF = (((0,), (0,)), ((), ()))

SHARD = 40
HALF = 80
PLANE = 160
NZ = 8
NX = 4
ROWS = NZ * PLANE
WIDE = 896
LANE = 128
ORDER = (0, 1, 7, 2, 6, 3, 5, 4)
POS = {s: i for i, s in enumerate(ORDER)}
NSEM = 232


def kernel(
    tok, cot, wg_h, wu_h, wd_h,
    gt_out, gwg_h, gwu_h, gwd_h,
    wg, wu, wd, tc, pf, pb, rb, sy, ry, own, hid,
    dpart, dsend, drecv, zsend, zrecv, zsum, acc, stage, xs, xr, fin, frecv,
    ss, rs, ls,
):
    row, col = lax.axis_index("row"), lax.axis_index("col")
    yh, x = row // NX, row % NX
    z, yl, k = col // 4, (col // 2) % 2, col % 2

    def at(dyh=0, dx=0, dz=0, dyl=0, dk=0):
        r = ((yh + dyh) % 2) * NX + (x + dx + NX) % NX
        c = ((z + dz + NZ) % NZ) * 4 + ((yl + dyl) % 2) * 2 + (k + dk) % 2
        return (r, c)

    def xi(d):
        return (x + d + NX) % NX

    count = [0]
    pending = []

    def send(src, dst, to, hold=True):
        i = count[0]
        count[0] += 1
        copy = pltpu.make_async_remote_copy(
            src_ref=src, dst_ref=dst, send_sem=ss.at[i], recv_sem=rs.at[i], device_id=to, device_id_type=MESH
        )
        copy.start()
        if hold:
            pending.append(copy)
        return copy

    loads = []
    for i, (src, dst) in enumerate(((wg_h, wg), (wu_h, wu), (wd_h, wd))):
        load = pltpu.make_async_copy(src, dst, ls.at[i])
        load.start()
        loads.append(load)

    partners = [at(dx=1), at(dx=-1), at(dyh=1), at(dk=1), at(dyl=1), at(dyl=1, dk=1)]
    partners += [at(dz=d) for d in range(1, NZ)]
    barrier = pltpu.get_barrier_semaphore()
    for p in partners:
        pl.semaphore_signal(barrier, inc=1, device_id=p, device_id_type=MESH)
    pl.semaphore_wait(barrier, len(partners))

    def rows(s, start, size):
        return pl.ds(pl.multiple_of(POS[s] * PLANE + start, 16), size)

    mine = jnp.where(k == 0, tok[...].astype(F32), cot[...].astype(F32))
    xs[...] = jnp.where(k == 0, cot[...].astype(F32), tok[...].astype(F32))
    first = send(xs, xr, at(dk=1))
    first.wait_recv()
    other = xr[...]
    low = jnp.where(k == 0, mine, other)
    high = jnp.where(k == 0, other, mine)
    both = jnp.concatenate([low, high], axis=0).astype(BF)
    tc[k, rows(0, yl * HALF, HALF), :] = both

    halves = (yl * HALF, (1 - yl) * HALF)
    ring = {}
    twin = {}

    def to_twin(s, h):
        ref = tc.at[k, rows(s, halves[h], HALF), :]
        twin[s, h] = send(ref, ref, at(dk=1))

    def to_ring(s, h, step):
        t = (s - step) % NZ
        src = tc.at[k, rows(s, halves[h], HALF), :]
        ring[t, h] = send(src, tc.at[k, rows(t, halves[h], HALF), :], at(dz=step))

    ref0 = tc.at[k, rows(0, halves[0], HALF), :]
    across = send(ref0, ref0, at(dyl=1))
    to_twin(0, 0)
    to_ring(0, 0, -1)
    to_ring(0, 0, 1)
    across.wait_recv()
    to_twin(0, 1)
    to_ring(0, 1, -1)
    to_ring(0, 1, 1)
    for load in loads:
        load.wait()

    def arrive(s):
        for h in (0, 1):
            ring[s, h].wait_recv()
            to_twin(s, h)
            if s in (1, 2) or (s == 3 and h == 0):
                to_ring(s, h, -1)
            if s in (7, 6) or (s == 5 and h == 1):
                to_ring(s, h, 1)

    def ways(s):
        return (1, -1, 1 if POS[s] % 2 == 0 else -1)

    b1, b2, by, cy, cx, cr, gy, dc, dz_ = {}, {}, {}, {}, {}, {}, {}, {}, {}

    def partial(s):
        for h in (0, 1):
            twin[s, h].wait_recv()
        t = tc[0, rows(s, 0, PLANE), :]
        c = tc[1, rows(s, 0, PLANE), :]
        r = rows(s, 0, PLANE)
        for a in range(3):
            if a == 0:
                v = jnp.dot(t, wg[...], preferred_element_type=F32)
            elif a == 1:
                v = jnp.dot(t, wu[...], preferred_element_type=F32)
            else:
                v = lax.dot_general(c, wd[...], LL, preferred_element_type=F32)
            for j in range(NX):
                piece = v[:, j * LANE : (j + 1) * LANE]
                pf[a, j, r, :] = piece
                pb[a, j, r, :] = piece.astype(BF)
            w = ways(s)[a]
            b1[s, a, 0] = send(pb.at[a, xi(2), r, :], rb.at[a, 0, r, :], at(dx=w))
            b1[s, a, 1] = send(pb.at[a, xi(-w), r, :], rb.at[a, 1, r, :], at(dx=-w))

    def relay(s):
        r = rows(s, 0, PLANE)
        for a in range(3):
            w = ways(s)[a]
            b1[s, a, 0].wait_recv()
            pb[a, xi(w), r, :] = (pf[a, xi(w), r, :] + rb[a, 0, r, :].astype(F32)).astype(BF)
            b2[s, a] = send(pb.at[a, xi(w), r, :], rb.at[a, 2, r, :], at(dx=w))

    def cross(s):
        i = POS[s]
        for a in range(3):
            b1[s, a, 1].wait_recv()
            b2[s, a].wait_recv()
            for h in (0, 1):
                r = rows(s, (yh if h == 0 else 1 - yh) * HALF, HALF)
                v = pf[a, x, r, :] + rb[a, 1, r, :].astype(F32) + rb[a, 2, r, :].astype(F32)
                if h == 0:
                    own[i, a] = v
                else:
                    sy[i, a] = v
        by[s] = send(sy.at[i], ry.at[i], at(dyh=1))

    def finish(s):
        i = POS[s]
        by[s].wait_recv()
        gate = own[i, 0] + ry[i, 0]
        up = own[i, 1] + ry[i, 1]
        back = own[i, 2] + ry[i, 2]
        sigma = 1.0 / (1.0 + jnp.exp(-gate))
        silu = gate * sigma
        r = rows(s, yh * HALF, HALF)
        hid[2, x, r, :] = (back * silu).astype(BF)
        w = ways(s)[2]
        src = hid.at[2, x, r, :]
        cx[s, 2, 0] = send(src, src, at(dx=w))
        cx[s, 2, 1] = send(src, src, at(dx=-w))
        hid[0, x, r, :] = (silu * up).astype(BF)
        hid[1, x, r, :] = (back * up * sigma * (1.0 + gate * (1.0 - sigma))).astype(BF)
        src = hid.at[pl.ds(0, 2), x, r, :]
        cy[s] = send(src, src, at(dyh=1))

    def spread(s):
        r = rows(s, 0, PLANE)
        rh = rows(s, yh * HALF, HALF)
        w = ways(s)[2]
        cx[s, 2, 0].wait_recv()
        src = hid.at[2, xi(-w), rh, :]
        cr[s, 2] = send(src, src, at(dx=w))
        cy[s].wait_recv()
        for a in (0, 1):
            w = ways(s)[a]
            src = hid.at[a, x, r, :]
            cx[s, a, 0] = send(src, src, at(dx=w))
            cx[s, a, 1] = send(src, src, at(dx=-w))

    def onward(s):
        r = rows(s, 0, PLANE)
        rh = rows(s, yh * HALF, HALF)
        for a in (0, 1):
            w = ways(s)[a]
            cx[s, a, 0].wait_recv()
            src = hid.at[a, xi(-w), r, :]
            cr[s, a] = send(src, src, at(dx=w))
        cx[s, 2, 1].wait_recv()
        cr[s, 2].wait_recv()
        src = hid.at[2, pl.ds(0, NX), rh, :]
        gy[s] = send(src, src, at(dyh=1))

    def wide(a, r):
        return jnp.concatenate([hid[a, j, r, :] for j in range(NX)], axis=1)

    def down(s):
        i = POS[s]
        r = rows(s, 0, PLANE)
        for a in (0, 1):
            cx[s, a, 1].wait_recv()
            cr[s, a].wait_recv()
        gy[s].wait_recv()
        v = lax.dot_general(wide(1, r), wg[...], LL, preferred_element_type=F32)
        v = v + lax.dot_general(wide(2, r), wu[...], LL, preferred_element_type=F32)
        dpart[i] = v
        dsend[i] = dpart[i, pl.ds(pl.multiple_of((1 - k) * HALF, 8), HALF), :]
        dc[s] = send(dsend.at[i], drecv.at[i], at(dk=1))

    def homeward(s):
        i = POS[s]
        dc[s].wait_recv()
        v = dpart[i, pl.ds(pl.multiple_of(k * HALF, 8), HALF), :] + drecv[i]
        if s == 0:
            zsum[...] = v
        else:
            zsend[i] = v.astype(BF)
            dz_[s] = send(zsend.at[i], zrecv.at[i], at(dz=s))

    def weights(part, last):
        n = ROWS // 2
        r = pl.ds(part * n, n)
        for a, (lhs, out) in enumerate(((None, gwd_h), (1, gwg_h), (2, gwu_h))):
            for j in range(2):
                if a == 0:
                    left = jnp.concatenate([hid[0, 2 * j, r, :], hid[0, 2 * j + 1, r, :]], axis=1)
                    v = lax.dot_general(left, tc[1, r, :], FF, preferred_element_type=F32)
                    place = (pl.ds(j * 256, 256), slice(None))
                    where = acc.at[0, pl.ds(j * 256, 256), :]
                else:
                    right = jnp.concatenate([hid[a, 2 * j, r, :], hid[a, 2 * j + 1, r, :]], axis=1)
                    v = lax.dot_general(right, tc[0, r, :], FF, preferred_element_type=F32)
                    where = acc.at[a, pl.ds(j * 256, 256), :]
                if last:
                    v = where[...] + v
                    if a == 0:
                        stage[0, pl.ds(j * 256, 256), :] = v.astype(BF)
                    else:
                        stage_t = v.T.astype(BF)
                        wstage = wg if a == 1 else wu
                        wstage[:, j * 256 : (j + 1) * 256] = stage_t
                else:
                    where[...] = v
            if last:
                src = stage.at[0] if a == 0 else (wg if a == 1 else wu)
                store = pltpu.make_async_copy(src, out, ls.at[a])
                store.start()
                stores.append(store)

    stores = []
    stages = [arrive, partial, relay, cross, finish, spread, onward, down, homeward]
    n = len(stages)
    for tick in range(NZ + n - 1):
        for j in reversed(range(n)):
            i = tick - j
            if 0 <= i < NZ:
                if not (j == 0 and ORDER[i] == 0):
                    stages[j](ORDER[i])
        if tick == n + 2:
            weights(0, False)
    weights(1, True)

    total = zsum[...]
    for s in ORDER[1:]:
        dz_[s].wait_recv()
        total = total + zrecv[POS[s]].astype(F32)
    fin[...] = total

    def tail(i, src, slot, to):
        return pltpu.make_async_remote_copy(
            src_ref=src, dst_ref=frecv.at[slot], send_sem=ss.at[NSEM + i], recv_sem=rs.at[NSEM + slot],
            device_id=to, device_id_type=MESH,
        )

    lows, highs = fin.at[pl.ds(0, SHARD), :], fin.at[pl.ds(SHARD, SHARD), :]
    home = yl == k
    near = tail(0, fin.at[pl.ds(pl.multiple_of((1 - k) * SHARD, 8), SHARD), :], 0, at(dk=1))
    ycol = z * 4 + (1 - yl) * 2
    far0 = tail(0, lows, 1, (row, ycol))
    far1 = tail(1, highs, 1, (row, ycol + 1))

    @pl.when(home)
    def _():
        near.start()
        far1.wait_recv()
        here = fin[pl.ds(pl.multiple_of(k * SHARD, 8), SHARD), :]
        gt_out[...] = (here + frecv[1]).astype(BF)
        near.wait_send()

    @pl.when(jnp.logical_not(home))
    def _():
        far0.start()
        far1.start()
        near.wait_recv()
        far1.wait_recv()
        gt_out[...] = (frecv[0] + frecv[1]).astype(BF)
        far0.wait_send()
        far1.wait_send()

    for copy in pending:
        copy.wait_send()
    for store in stores:
        store.wait()


def local(tokens, cotangent, w_gate, w_up, w_down):
    vm = pl.BlockSpec(memory_space=pltpu.VMEM)
    hbm = pl.BlockSpec(memory_space=pl.ANY)
    V = pltpu.VMEM
    return pl.pallas_call(
        kernel,
        out_shape=[
            jax.ShapeDtypeStruct((SHARD, WIDE), BF),
            jax.ShapeDtypeStruct((WIDE, 512), BF),
            jax.ShapeDtypeStruct((WIDE, 512), BF),
            jax.ShapeDtypeStruct((512, WIDE), BF),
        ],
        in_specs=[vm, vm, hbm, hbm, hbm],
        out_specs=[vm, hbm, hbm, hbm],
        scratch_shapes=[
            V((WIDE, 512), BF), V((WIDE, 512), BF), V((512, WIDE), BF),
            V((2, ROWS, WIDE), BF),
            V((3, NX, ROWS, LANE), F32),
            V((3, NX, ROWS, LANE), BF),
            V((3, 3, ROWS, LANE), BF),
            V((NZ, 3, HALF, LANE), F32),
            V((NZ, 3, HALF, LANE), F32),
            V((NZ, 3, HALF, LANE), F32),
            V((3, NX, ROWS, LANE), BF),
            V((NZ, PLANE, WIDE), F32),
            V((NZ, HALF, WIDE), F32),
            V((NZ, HALF, WIDE), F32),
            V((NZ, HALF, WIDE), BF),
            V((NZ, HALF, WIDE), BF),
            V((HALF, WIDE), F32),
            V((3, 512, WIDE), F32),
            V((1, 512, WIDE), BF),
            V((SHARD, WIDE), F32), V((SHARD, WIDE), F32),
            V((HALF, WIDE), F32), V((2, SHARD, WIDE), F32),
            pltpu.SemaphoreType.DMA((NSEM + 2,)),
            pltpu.SemaphoreType.DMA((NSEM + 2,)),
            pltpu.SemaphoreType.DMA((3,)),
        ],
        compiler_params=pltpu.CompilerParams(
            collective_id=0, has_side_effects=True, vmem_limit_bytes=62 * 2**20
        ),
        name="ffn_backward",
    )(tokens, cotangent, w_gate, w_up, w_down)


def solution(mesh):
    return jax.shard_map(
        local,
        mesh=mesh,
        in_specs=(P("col", "row"), P("col", "row"), P("row", "col"), P("row", "col"), P("col", "row")),
        out_specs=(P("col", "row"), P("row", "col"), P("row", "col"), P("col", "row")),
        check_vma=False,
    )
```

time: 582 us -> 122 us (0.21)
  the two profiles are of different devices: /device:TPU:1 before, /device:TPU:97 now
where the time goes in v1:
time: 122 us
  Pallas kernels  115 us (94%)
  local copies, waits for them, and re-layouts  6.2 us (5%)
    pallas_call x1, Pallas kernels, local(): pl.pallas_call(kernel, out_shape=[jax.ShapeDtypeStruct((SHARD, WIDE), BF)...  115 us
    unnamed x8, local copies, waits for them, and re-layouts  6.2 us

profile of v1, /device:TPU:97, one launch (start us, length us, event | category | flops | bytes accessed | tf_op | source)
XLA Modules:
  0.0 121.6 jit_solution(6711698248371309957)
XLA Ops:
  0.6 114.7 %ffn_backward.1 = (bf16[40,896]{1,0:T(8,128)(2,1)}, bf16[896,512]{1,0:T(8,128)(2,1)}, bf16[896,512]{1,0:T(8,128)(2,1)}, bf16[512,896]{1,0:T(8,128)(2,1)}) custom-call(bf16[40,896]{1,0:T(8,128)(2,1)} %tok.1, bf16[40,896]{1,0:T(8,128)(2,1)} %cot.1, bf16[896,512]{1,0:T(8,128)(2,1)} %wg_h.1, bf16[896,512]{1,0:T(8,128)(2,1)} %wu_h.1, bf16[512,896]{1,0:T(8,128)(2,1)} %wd_h.1), custom_call_target="tpu_custom_call" | custom-call | tf_op jit(solution)/shard_map/ffn_backward/pallas_call | solution.py:330
  115.4 1.5 %copy.13 = bf16[40,896]{1,0:T(8,128)(2,1)} copy(bf16[40,896]{1,0:T(8,128)(2,1)} %get-tuple-element.8) | data formatting | bytes 143360
  116.9 0.0 copy-start.1
  116.9 2.2 %copy.14 = bf16[896,512]{1,0:T(8,128)(2,1)} copy(bf16[896,512]{1,0:T(8,128)(2,1)} %get-tuple-element.9) | data formatting | bytes 1835008
  119.1 0.0 copy-done.1
  119.2 0.0 copy-start
  119.2 0.9 copy.15
  120.1 0.6 copy-done
  120.7 0.9 copy.16
Async XLA Ops:
  116.9 2.2 %copy-start.1 = (bf16[896,512]{1,0:T(8,128)(2,1)S(1)}, bf16[896,512]{1,0:T(8,128)(2,1)}, u32[]{:S(2)}) copy-start(bf16[896,512]{1,0:T(8,128)(2,1)} %get-tuple-element.10) | copy-start | bytes 2752516
  119.2 1.5 %copy-start = (bf16[512,896]{1,0:T(8,128)(2,1)S(1)}, bf16[512,896]{1,0:T(8,128)(2,1)}, u32[]{:S(2)}) copy-start(bf16[512,896]{1,0:T(8,128)(2,1)} %get-tuple-element.11) | copy-start | bytes 2752516

commit v2 on v1

v2 whole, which is shorter than its diff:
```python
import jax
import jax.numpy as jnp
from jax import lax
from jax.experimental import pallas as pl
from jax.experimental.pallas import tpu as pltpu
from jax.sharding import PartitionSpec as P

MESH = pl.DeviceIdType.MESH
BF = jnp.bfloat16
F32 = jnp.float32
LL = (((1,), (1,)), ((), ()))
FF = (((0,), (0,)), ((), ()))

SHARD = 40
HALF = 80
PLANE = 160
NZ = 8
NX = 4
ROWS = NZ * PLANE
WIDE = 896
LANE = 128
NSEM = 280
DOWN = (1, 7, 2, 6, 3, 5, 4, 0)
POS = {s: i for i, s in enumerate(DOWN)}
PATHS = {0: (), 1: (2,), 2: (2,), 3: (2,), 4: (2,), 5: (2,), 6: (2,), 7: (2,)}
DIRECT = ()
PROGRAM = (
    ('partial', 0, 0),
    ('start2',),
    ('arrive', 1, 0),
    ('arrive', 7, 0),
    ('partial', 0, 1),
    ('relay', 0, 0),
    ('relay', 0, 1),
    ('arrive', 7, 1),
    ('arrive', 1, 1),
    ('relay', 0, 2),
    ('partial', 7),
    ('partial', 1),
    ('arrive', 2, 0),
    ('arrive', 6, 0),
    ('cross', 0),
    ('relay', 7, 0),
    ('arrive', 6, 1),
    ('arrive', 2, 1),
    ('relay', 7, 1),
    ('relay', 7, 2),
    ('partial', 6),
    ('relay', 1, 0),
    ('partial', 2),
    ('relay', 1, 1),
    ('arrive', 3, 0),
    ('arrive', 5, 0),
    ('relay', 1, 2),
    ('cross', 7),
    ('arrive', 3, 1),
    ('arrive', 5, 1),
    ('relay', 6, 0),
    ('relay', 6, 1),
    ('partial', 3),
    ('relay', 6, 2),
    ('partial', 5),
    ('relay', 2, 1),
    ('arrive', 4, 0),
    ('relay', 2, 0),
    ('relay', 2, 2),
    ('cross', 1),
    ('arrive', 4, 1),
    ('finish', 7),
    ('relay', 3, 0),
    ('partial', 4),
    ('relay', 3, 1),
    ('relay', 3, 2),
    ('cross', 6),
    ('relay', 5, 0),
    ('relay', 5, 1),
    ('finish', 1),
    ('relay', 5, 2),
    ('spreadB', 7),
    ('cross', 2),
    ('finish', 0),
    ('spreadA', 7, 2),
    ('relay', 4, 0),
    ('relay', 4, 1),
    ('relay', 4, 2),
    ('finish', 6),
    ('spreadB', 1),
    ('cross', 3),
    ('cross', 5),
    ('spreadA', 1, 2),
    ('finish', 2),
    ('onward', 7, 0),
    ('onward', 7, 1),
    ('spreadB', 0),
    ('onwardY', 7),
    ('spreadB', 6),
    ('spreadA', 6, 2),
    ('cross', 4),
    ('onward', 1, 0),
    ('finish', 3),
    ('onward', 1, 1),
    ('onwardY', 1),
    ('spreadA', 2, 2),
    ('onward', 0, 0),
    ('finish', 5),
    ('spreadB', 2),
    ('onward', 0, 2),
    ('onward', 0, 1),
    ('onward', 6, 0),
    ('onwardY', 6),
    ('onward', 6, 1),
    ('spreadA', 3, 2),
    ('finish', 4),
    ('onwardY', 2),
    ('spreadA', 5, 2),
    ('spreadB', 3),
    ('onward', 2, 0),
    ('onward', 2, 1),
    ('down', 1),
    ('down', 7),
    ('spreadB', 5),
    ('onwardY', 3),
    ('onwardY', 5),
    ('spreadA', 4, 2),
    ('homeward', 1),
    ('homeward', 7),
    ('onward', 3, 0),
    ('spreadB', 4),
    ('onward', 3, 1),
    ('down', 2),
    ('down', 6),
    ('onward', 5, 0),
    ('onward', 5, 1),
    ('onwardY', 4),
    ('homeward', 2),
    ('homeward', 6),
    ('onward', 4, 0),
    ('onward', 4, 1),
    ('depart', 1),
    ('down', 3),
    ('down', 5),
    ('depart', 7),
    ('homeward', 3),
    ('homeward', 5),
    ('down', 4),
    ('depart', 2),
    ('down', 0),
    ('depart', 6),
    ('homeward', 4),
    ('homeward', 0),
    ('depart', 3),
    ('depart', 5),
    ('weights', 0, 4, True, False),
    ('depart', 4),
    ('depart', 0),
    ('fin',),
    ('weights', 4, 4, False, True),
)


def kernel(
    tok, cot, wg_h, wu_h, wd_h,
    gt_out, gwg_h, gwu_h, gwd_h,
    wg, wu, wd, tc, pf, pb, rb, sy, ry, own, hid,
    dpart, dsend, drecv, zsend, zrecv, zhome, zsum, acc, stage, xs, xr, fin, frecv,
    ss, rs, ls,
):
    row, col = lax.axis_index("row"), lax.axis_index("col")
    yh, x = row // NX, row % NX
    z, yl, k = col // 4, (col // 2) % 2, col % 2

    def at(dyh=0, dx=0, dz=0, dyl=0, dk=0):
        r = ((yh + dyh) % 2) * NX + (x + dx + NX) % NX
        c = ((z + dz + NZ) % NZ) * 4 + ((yl + dyl) % 2) * 2 + (k + dk) % 2
        return (r, c)

    def xi(d):
        return (x + d + NX) % NX

    count = [0]
    pending = []

    def send(src, dst, to, hold=True):
        i = count[0]
        count[0] += 1
        copy = pltpu.make_async_remote_copy(
            src_ref=src, dst_ref=dst, send_sem=ss.at[i], recv_sem=rs.at[i], device_id=to, device_id_type=MESH
        )
        copy.start()
        if hold:
            pending.append(copy)
        return copy

    loads = []
    for i, (src, dst) in enumerate(((wg_h, wg), (wu_h, wu), (wd_h, wd))):
        load = pltpu.make_async_copy(src, dst, ls.at[i])
        load.start()
        loads.append(load)

    partners = [at(dx=1), at(dx=-1), at(dx=2), at(dyh=1), at(dk=1), at(dyl=1)]
    partners += [at(dz=d) for d in range(1, NZ)]
    barrier = pltpu.get_barrier_semaphore()
    for p in partners:
        pl.semaphore_signal(barrier, inc=1, device_id=p, device_id_type=MESH)
    pl.semaphore_wait(barrier, len(partners))

    def rows(s, start, size):
        return pl.ds(pl.multiple_of(POS[s] * PLANE + start, 16), size)

    mine = jnp.where(k == 0, tok[...].astype(F32), cot[...].astype(F32))
    xs[...] = jnp.where(k == 0, cot[...].astype(F32), tok[...].astype(F32))
    first = send(xs, xr, at(dk=1))
    first.wait_recv()
    other = xr[...]
    low = jnp.where(k == 0, mine, other)
    high = jnp.where(k == 0, other, mine)
    both = jnp.concatenate([low, high], axis=0).astype(BF)
    tc[k, rows(0, yl * HALF, HALF), :] = both

    halves = (yl * HALF, (1 - yl) * HALF)
    ring = {}
    twin = {}

    def to_twin(s, h):
        ref = tc.at[k, rows(s, halves[h], HALF), :]
        twin[s, h] = send(ref, ref, at(dk=1))

    def to_ring(s, h, step):
        t = (s - step) % NZ
        src = tc.at[k, rows(s, halves[h], HALF), :]
        ring[t, h] = send(src, tc.at[k, rows(t, halves[h], HALF), :], at(dz=step))

    ref0 = tc.at[k, rows(0, halves[0], HALF), :]
    across = send(ref0, ref0, at(dyl=1))
    to_twin(0, 0)
    to_ring(0, 0, -1)
    to_ring(0, 0, 1)
    def start2():
        across.wait_recv()
        to_twin(0, 1)
        to_ring(0, 1, -1)
        to_ring(0, 1, 1)

    for load in loads:
        load.wait()

    def arrive(s, h):
        ring[s, h].wait_recv()
        to_twin(s, h)
        if s in (1, 2) or (s == 3 and h == 0):
            to_ring(s, h, -1)
        if s in (7, 6) or (s == 5 and h == 1):
            to_ring(s, h, 1)

    def ways(s):
        return (1, -1, 1 if POS[s] % 2 == 0 else -1)

    b1, b2, by, cy, cx, cr, gy, dc, yh_, dz_ = {}, {}, {}, {}, {}, {}, {}, {}, {}, {}
    home = yl == k

    def partial(s, half=None):
        for h in (0, 1) if half is None else (half,):
            twin[s, h].wait_recv()
        r = rows(s, 0, PLANE) if half is None else rows(s, halves[half], HALF)
        t = tc[0, r, :]
        c = tc[1, r, :]
        for a in range(3):
            if a == 0:
                v = jnp.dot(t, wg[...], preferred_element_type=F32)
            elif a == 1:
                v = jnp.dot(t, wu[...], preferred_element_type=F32)
            else:
                v = lax.dot_general(c, wd[...], LL, preferred_element_type=F32)
            for j in range(NX):
                piece = v[:, j * LANE : (j + 1) * LANE]
                pf[a, j, r, :] = piece
                pb[a, j, r, :] = piece.astype(BF)
            w = ways(s)[a]
            if s in DIRECT:
                plan = ((0, w, w), (1, -w, -w), (2, 2, 2))
            else:
                plan = ((0, 2, w), (1, -w, -w))
            for slot, block, to in plan:
                copy = send(pb.at[a, xi(block), r, :], rb.at[a, slot, r, :], at(dx=to))
                b1.setdefault((s, a, slot), []).append(copy)

    def relay(s, a):
        r = rows(s, 0, PLANE)
        w = ways(s)[a]
        for copy in b1[s, a, 0]:
            copy.wait_recv()
        pb[a, xi(w), r, :] = (pf[a, xi(w), r, :] + rb[a, 0, r, :].astype(F32)).astype(BF)
        b2[s, a] = send(pb.at[a, xi(w), r, :], rb.at[a, 2, r, :], at(dx=w))

    def cross(s):
        i = POS[s]
        for a in range(3):
            for slot in (0, 1, 2) if s in DIRECT else (1,):
                for copy in b1[s, a, slot]:
                    copy.wait_recv()
            if s not in DIRECT:
                b2[s, a].wait_recv()
            for h in (0, 1):
                r = rows(s, (yh if h == 0 else 1 - yh) * HALF, HALF)
                v = pf[a, x, r, :] + rb[a, 1, r, :].astype(F32) + rb[a, 2, r, :].astype(F32)
                if s in DIRECT:
                    v = v + rb[a, 0, r, :].astype(F32)
                if h == 0:
                    own[i, a] = v
                else:
                    sy[i, a] = v
        by[s] = send(sy.at[i], ry.at[i], at(dyh=1))

    def finish(s):
        i = POS[s]
        by[s].wait_recv()
        gate = own[i, 0] + ry[i, 0]
        up = own[i, 1] + ry[i, 1]
        back = own[i, 2] + ry[i, 2]
        sigma = 1.0 / (1.0 + jnp.exp(-gate))
        silu = gate * sigma
        r = rows(s, yh * HALF, HALF)
        hid[2, x, r, :] = (back * silu).astype(BF)
        hid[0, x, r, :] = (silu * up).astype(BF)
        hid[1, x, r, :] = (back * up * sigma * (1.0 + gate * (1.0 - sigma))).astype(BF)
        for a in PATHS[s]:
            w = ways(s)[a]
            src = hid.at[a, x, r, :]
            cx[s, a, 0] = send(src, src, at(dx=w))
            cx[s, a, 1] = send(src, src, at(dx=-w))
            if s in DIRECT:
                cr[s, a] = send(src, src, at(dx=2))
        n = 3 - len(PATHS[s])
        if n:
            src = hid.at[pl.ds(0, n), x, r, :]
            cy[s] = send(src, src, at(dyh=1))

    def spreadA(s, a):
        w = ways(s)[a]
        cx[s, a, 0].wait_recv()
        src = hid.at[a, xi(-w), rows(s, yh * HALF, HALF), :]
        cr[s, a] = send(src, src, at(dx=w))

    def spreadB(s):
        r = rows(s, 0, PLANE)
        cy[s].wait_recv()
        for a in range(3 - len(PATHS[s])):
            w = ways(s)[a]
            src = hid.at[a, x, r, :]
            cx[s, a, 0] = send(src, src, at(dx=w))
            cx[s, a, 1] = send(src, src, at(dx=-w))
            if s in DIRECT:
                cr[s, a] = send(src, src, at(dx=2))

    def onward(s, a):
        w = ways(s)[a]
        cx[s, a, 0].wait_recv()
        src = hid.at[a, xi(-w), rows(s, 0, PLANE), :]
        cr[s, a] = send(src, src, at(dx=w))

    def onwardY(s):
        for a in PATHS[s]:
            if s in DIRECT:
                cx[s, a, 0].wait_recv()
            cx[s, a, 1].wait_recv()
            cr[s, a].wait_recv()
        n = len(PATHS[s])
        src = hid.at[pl.ds(3 - n, n), pl.ds(0, NX), rows(s, yh * HALF, HALF), :]
        gy[s] = send(src, src, at(dyh=1))

    def wide(a, r):
        return jnp.concatenate([hid[a, j, r, :] for j in range(NX)], axis=1)

    def down(s):
        i = POS[s]
        r = rows(s, 0, PLANE)
        for a in range(3 - len(PATHS[s])):
            if s in DIRECT:
                cx[s, a, 0].wait_recv()
            cx[s, a, 1].wait_recv()
            cr[s, a].wait_recv()
        if PATHS[s]:
            gy[s].wait_recv()
        v = lax.dot_general(wide(1, r), wg[...], LL, preferred_element_type=F32)
        v = v + lax.dot_general(wide(2, r), wu[...], LL, preferred_element_type=F32)
        dpart[i] = v
        dsend[i] = dpart[i, pl.ds(pl.multiple_of((1 - k) * HALF, 8), HALF), :]
        dc[s] = send(dsend.at[i], drecv.at[i], at(dk=1))

    def homeward(s):
        i = POS[s]
        dc[s].wait_recv()
        v = dpart[i, pl.ds(pl.multiple_of(k * HALF, 8), HALF), :] + drecv[i]
        zsend[i] = v.astype(BF)
        dpart[i, 0:HALF, :] = v
        index = (count[0], count[0] + 1)
        count[0] += 2
        over = pltpu.make_async_remote_copy(
            src_ref=zsend.at[i], dst_ref=zrecv.at[i], send_sem=ss.at[index[0]], recv_sem=rs.at[index[0]],
            device_id=at(dyl=1), device_id_type=MESH,
        )
        yh_[s] = over, index[1]

        @pl.when(jnp.logical_not(home))
        def _():
            over.start()

    def depart(s):
        i = POS[s]
        over, index = yh_[s]
        if s:
            go = pltpu.make_async_remote_copy(
                src_ref=zsend.at[i], dst_ref=zhome.at[i], send_sem=ss.at[index], recv_sem=rs.at[index],
                device_id=at(dz=s), device_id_type=MESH,
            )
            dz_[s] = go

        @pl.when(home)
        def _():
            over.wait_recv()
            v = dpart[i, 0:HALF, :] + zrecv[i].astype(F32)
            if s == 0:
                zsum[...] = v
            else:
                zsend[i] = v.astype(BF)
                go.start()

        @pl.when(jnp.logical_not(home))
        def _():
            over.wait_send()

    def weights(first, count, start, last):
        n = count * PLANE
        r = pl.ds(first * PLANE, n)
        for a, out in enumerate((gwd_h, gwg_h, gwu_h)):
            for j in range(2):
                pair = jnp.concatenate([hid[a, 2 * j, r, :], hid[a, 2 * j + 1, r, :]], axis=1)
                v = lax.dot_general(pair, tc[1 if a == 0 else 0, r, :], FF, preferred_element_type=F32)
                where = acc.at[a, pl.ds(j * 256, 256), :]
                if not start:
                    v = where[...] + v
                if not last:
                    where[...] = v
                elif a == 0:
                    stage[0, pl.ds(j * 256, 256), :] = v.astype(BF)
                else:
                    (wg if a == 1 else wu)[:, j * 256 : (j + 1) * 256] = v.T.astype(BF)
            if last:
                src = stage.at[0] if a == 0 else (wg if a == 1 else wu)
                store = pltpu.make_async_copy(src, out, ls.at[a])
                store.start()
                stores.append(store)

    near = pltpu.make_async_remote_copy(
        src_ref=fin.at[pl.ds(pl.multiple_of((1 - k) * SHARD, 8), SHARD), :], dst_ref=frecv,
        send_sem=ss.at[NSEM], recv_sem=rs.at[NSEM], device_id=at(dk=1), device_id_type=MESH,
    )

    def fin_send():
        @pl.when(home)
        def _():
            total = zsum[...]
            for s in dz_:
                dz_[s].wait_recv()
                total = total + zhome[POS[s]].astype(F32)
            fin[...] = total
            near.start()

    stores = []
    table = dict(
        start2=start2,
        arrive=arrive, partial=partial, relay=relay, cross=cross, finish=finish, spreadA=spreadA, spreadB=spreadB,
        onward=onward, onwardY=onwardY, down=down, homeward=homeward, depart=depart, weights=weights, fin=fin_send,
    )
    for name, *where in PROGRAM:
        table[name](*where)

    @pl.when(home)
    def _():
        gt_out[...] = fin[pl.ds(pl.multiple_of(k * SHARD, 8), SHARD), :].astype(BF)
        near.wait_send()
        for s in dz_:
            dz_[s].wait_send()

    @pl.when(jnp.logical_not(home))
    def _():
        near.wait_recv()
        gt_out[...] = frecv[...].astype(BF)

    for copy in pending:
        copy.wait_send()
    for store in stores:
        store.wait()


def hand_over(g_in, a_in, b_in, c_in, g_out, a_out, b_out, c_out, a, b, c, into, out):
    stays = ((a_in, a, a_out), (b_in, b, b_out), (c_in, c, c_out))
    first = [pltpu.make_async_copy(src, via, into.at[i]) for i, (src, via, _) in enumerate(stays)]
    second = [pltpu.make_async_copy(via, dst, out.at[i]) for i, (_, via, dst) in enumerate(stays)]
    for copy in first:
        copy.start()
    g_out[...] = g_in[...]
    for before, after in zip(first, second):
        before.wait()
        after.start()
    for copy in second:
        copy.wait()


def local(tokens, cotangent, w_gate, w_up, w_down):
    vm = pl.BlockSpec(memory_space=pltpu.VMEM)
    hbm = pl.BlockSpec(memory_space=pl.ANY)
    V = pltpu.VMEM
    shapes = [jax.ShapeDtypeStruct(s, BF) for s in ((SHARD, WIDE), (WIDE, 512), (WIDE, 512), (512, WIDE))]
    grads = pl.pallas_call(
        kernel,
        out_shape=shapes,
        in_specs=[vm, vm, hbm, hbm, hbm],
        out_specs=[vm, hbm, hbm, hbm],
        scratch_shapes=[
            V((WIDE, 512), BF), V((WIDE, 512), BF), V((512, WIDE), BF),
            V((2, ROWS, WIDE), BF),
            V((3, NX, ROWS, LANE), F32),
            V((3, NX, ROWS, LANE), BF),
            V((3, 3, ROWS, LANE), BF),
            V((NZ, 3, HALF, LANE), F32),
            V((NZ, 3, HALF, LANE), F32),
            V((NZ, 3, HALF, LANE), F32),
            V((3, NX, ROWS, LANE), BF),
            V((NZ, PLANE, WIDE), F32),
            V((NZ, HALF, WIDE), F32),
            V((NZ, HALF, WIDE), F32),
            V((NZ, HALF, WIDE), BF),
            V((NZ, HALF, WIDE), BF),
            V((NZ, HALF, WIDE), BF),
            V((HALF, WIDE), F32),
            V((3, 512, WIDE), F32),
            V((1, 512, WIDE), BF),
            V((SHARD, WIDE), F32), V((SHARD, WIDE), F32),
            V((HALF, WIDE), F32), V((SHARD, WIDE), F32),
            pltpu.SemaphoreType.DMA((NSEM + 1,)),
            pltpu.SemaphoreType.DMA((NSEM + 1,)),
            pltpu.SemaphoreType.DMA((3,)),
        ],
        compiler_params=pltpu.CompilerParams(
            collective_id=0, has_side_effects=True, vmem_limit_bytes=62 * 2**20
        ),
        name="ffn_backward",
    )(tokens, cotangent, w_gate, w_up, w_down)
    return pl.pallas_call(
        hand_over,
        out_shape=shapes,
        in_specs=[vm, hbm, hbm, hbm],
        out_specs=[vm, hbm, hbm, hbm],
        scratch_shapes=[V(s.shape, BF) for s in shapes[1:]] + [pltpu.SemaphoreType.DMA((3,))] * 2,
        name="hand_over",
    )(*grads)


def solution(mesh):
    return jax.shard_map(
        local,
        mesh=mesh,
        in_specs=(P("col", "row"), P("col", "row"), P("row", "col"), P("row", "col"), P("col", "row")),
        out_specs=(P("col", "row"), P("row", "col"), P("row", "col"), P("col", "row")),
        check_vma=False,
    )
```

time: 122 us -> 113 us (0.926)
  the two profiles are of different devices: /device:TPU:97 before, /device:TPU:1 now
where the time goes in v2:
time: 113 us; the launch traced here: 112 us
  Pallas kernels  112 us (99%)
    pallas_call x1, Pallas kernels, local(): pl.pallas_call(kernel, out_shape=shapes, in_specs=[vm, vm, hbm, hbm, hbm]...  107 us
    pallas_call x1, Pallas kernels, local(): pl.pallas_call(hand_over, out_shape=shapes, in_specs=[vm, hbm, hbm, hbm],...  4.27 us

profile of v2, /device:TPU:1, one launch (start us, length us, event | category | flops | bytes accessed | tf_op | source)
XLA Modules:
  0.0 112.3 jit_solution(6724773459106060250)
XLA Ops:
  0.6 107.3 %ffn_backward.1 = (bf16[40,896]{1,0:T(8,128)(2,1)}, bf16[896,512]{1,0:T(8,128)(2,1)}, bf16[896,512]{1,0:T(8,128)(2,1)}, bf16[512,896]{1,0:T(8,128)(2,1)}) custom-call(bf16[40,896]{1,0:T(8,128)(2,1)} %tok.1, bf16[40,896]{1,0:T(8,128)(2,1)} %cot.1, bf16[896,512]{1,0:T(8,128)(2,1)} %wg_h.1, bf16[896,512]{1,0:T(8,128)(2,1)} %wu_h.1, bf16[512,896]{1,0:T(8,128)(2,1)} %wd_h.1), custom_call_target="tpu_custom_call" | custom-call | tf_op jit(solution)/shard_map/ffn_backward/pallas_call | solution.py:515
  107.9 4.3 %hand_over.1 = (bf16[40,896]{1,0:T(8,128)(2,1)}, bf16[896,512]{1,0:T(8,128)(2,1)}, bf16[896,512]{1,0:T(8,128)(2,1)}, bf16[512,896]{1,0:T(8,128)(2,1)}) custom-call(bf16[40,896]{1,0:T(8,128)(2,1)} %get-tuple-element.8.g_in, bf16[896,512]{1,0:T(8,128)(2,1)} %get-tuple-element.9.a_in, bf16[896,512]{1,0:T(8,128)(2,1)} %get-tuple-element.10.b_in, ...), custom_call_target="tpu_custom_call" | custom-call | tf_op jit(solution)/shard_map/hand_over/pallas_call | solution.py:550

commit v3 on v2

--- a/solution.py
+++ b/solution.py
@@ -27,134 +27,138 @@
 PROGRAM = (
     ('partial', 0, 0),
     ('start2',),
+    ('arrive', 7, 0),
     ('arrive', 1, 0),
-    ('arrive', 7, 0),
     ('partial', 0, 1),
+    ('arrive', 7, 1),
+    ('relay', 0, 2),
+    ('arrive', 1, 1),
     ('relay', 0, 0),
+    ('partial', 7),
+    ('arrive', 6, 0),
+    ('partial', 1),
+    ('arrive', 6, 1),
+    ('arrive', 2, 0),
     ('relay', 0, 1),
-    ('arrive', 7, 1),
-    ('arrive', 1, 1),
-    ('relay', 0, 2),
-    ('partial', 7),
-    ('partial', 1),
-    ('arrive', 2, 0),
-    ('arrive', 6, 0),
+    ('partial', 6),
+    ('relay', 7, 2),
+    ('arrive', 5, 0),
+    ('arrive', 2, 1),
+    ('relay', 1, 0),
+    ('relay', 7, 0),
+    ('relay', 1, 1),
+    ('relay', 1, 2),
+    ('arrive', 5, 1),
+    ('arrive', 3, 0),
+    ('relay', 6, 0),
     ('cross', 0),
-    ('relay', 7, 0),
-    ('arrive', 6, 1),
-    ('arrive', 2, 1),
+    ('relay', 6, 1),
     ('relay', 7, 1),
-    ('relay', 7, 2),
-    ('partial', 6),
-    ('relay', 1, 0),
-    ('partial', 2),
-    ('relay', 1, 1),
-    ('arrive', 3, 0),
-    ('arrive', 5, 0),
-    ('relay', 1, 2),
+    ('partial', 5),
+    ('arrive', 3, 1),
+    ('cross', 1),
+    ('relay', 6, 2),
+    ('partial', 3),
     ('cross', 7),
-    ('arrive', 3, 1),
-    ('arrive', 5, 1),
-    ('relay', 6, 0),
-    ('relay', 6, 1),
-    ('partial', 3),
-    ('relay', 6, 2),
-    ('partial', 5),
-    ('relay', 2, 1),
+    ('relay', 5, 0),
     ('arrive', 4, 0),
-    ('relay', 2, 0),
-    ('relay', 2, 2),
-    ('cross', 1),
     ('arrive', 4, 1),
-    ('finish', 7),
-    ('relay', 3, 0),
+    ('relay', 5, 1),
+    ('relay', 5, 2),
+    ('cross', 6),
     ('partial', 4),
     ('relay', 3, 1),
     ('relay', 3, 2),
-    ('cross', 6),
-    ('relay', 5, 0),
-    ('relay', 5, 1),
+    ('relay', 3, 0),
+    ('finish', 0),
+    ('partial', 2),
     ('finish', 1),
-    ('relay', 5, 2),
+    ('cross', 5),
+    ('relay', 4, 2),
+    ('relay', 4, 1),
+    ('relay', 4, 0),
+    ('finish', 6),
+    ('cross', 3),
+    ('finish', 7),
+    ('relay', 2, 0),
+    ('relay', 2, 1),
+    ('spreadA', 1, 2),
+    ('relay', 2, 2),
+    ('spreadB', 1),
+    ('finish', 5),
+    ('cross', 4),
+    ('spreadA', 7, 2),
+    ('spreadB', 6),
+    ('finish', 3),
     ('spreadB', 7),
     ('cross', 2),
-    ('finish', 0),
-    ('spreadA', 7, 2),
-    ('relay', 4, 0),
-    ('relay', 4, 1),
-    ('relay', 4, 2),
-    ('finish', 6),
-    ('spreadB', 1),
-    ('cross', 3),
-    ('cross', 5),
-    ('spreadA', 1, 2),
+    ('spreadA', 6, 2),
+    ('onwardY', 7),
+    ('spreadB', 5),
+    ('spreadA', 3, 2),
+    ('spreadA', 5, 2),
+    ('onward', 1, 1),
+    ('onward', 1, 0),
+    ('finish', 4),
+    ('onwardY', 6),
+    ('spreadB', 3),
     ('finish', 2),
-    ('onward', 7, 0),
-    ('onward', 7, 1),
-    ('spreadB', 0),
-    ('onwardY', 7),
-    ('spreadB', 6),
-    ('spreadA', 6, 2),
-    ('cross', 4),
-    ('onward', 1, 0),
-    ('finish', 3),
-    ('onward', 1, 1),
-    ('onwardY', 1),
-    ('spreadA', 2, 2),
-    ('onward', 0, 0),
-    ('finish', 5),
-    ('spreadB', 2),
-    ('onward', 0, 2),
-    ('onward', 0, 1),
-    ('onward', 6, 0),
-    ('onwardY', 6),
-    ('onward', 6, 1),
-    ('spreadA', 3, 2),
-    ('finish', 4),
-    ('onwardY', 2),
-    ('spreadA', 5, 2),
-    ('spreadB', 3),
-    ('onward', 2, 0),
-    ('onward', 2, 1),
-    ('down', 1),
-    ('down', 7),
-    ('spreadB', 5),
-    ('onwardY', 3),
     ('onwardY', 5),
-    ('spreadA', 4, 2),
-    ('homeward', 1),
-    ('homeward', 7),
-    ('onward', 3, 0),
-    ('spreadB', 4),
-    ('onward', 3, 1),
-    ('down', 2),
-    ('down', 6),
     ('onward', 5, 0),
     ('onward', 5, 1),
+    ('onward', 6, 0),
+    ('spreadA', 4, 2),
+    ('onward', 3, 0),
+    ('onwardY', 3),
+    ('spreadB', 4),
+    ('spreadA', 2, 2),
+    ('onward', 3, 1),
+    ('onwardY', 1),
     ('onwardY', 4),
-    ('homeward', 2),
-    ('homeward', 6),
+    ('spreadB', 2),
+    ('onward', 7, 1),
+    ('down', 5),
     ('onward', 4, 0),
     ('onward', 4, 1),
-    ('depart', 1),
+    ('onwardY', 2),
+    ('onward', 6, 1),
+    ('onward', 7, 0),
+    ('spreadB', 0),
     ('down', 3),
-    ('down', 5),
-    ('depart', 7),
+    ('homeward', 5),
+    ('down', 1),
     ('homeward', 3),
-    ('homeward', 5),
+    ('onward', 2, 1),
+    ('onward', 2, 0),
     ('down', 4),
+    ('homeward', 1),
+    ('down', 7),
+    ('depart', 5),
+    ('down', 6),
+    ('homeward', 4),
+    ('depart', 3),
+    ('onward', 0, 2),
+    ('down', 2),
+    ('homeward', 6),
+    ('homeward', 2),
+    ('depart', 4),
+    ('onward', 0, 0),
+    ('onward', 0, 1),
+    ('weights', 0, 4, True, False, 0),
+    ('homeward', 7),
+    ('depart', 6),
+    ('weights', 0, 4, True, False, 1),
     ('depart', 2),
     ('down', 0),
-    ('depart', 6),
-    ('homeward', 4),
+    ('depart', 7),
+    ('weights', 0, 4, True, False, 2),
+    ('weights', 4, 4, False, True, 0),
     ('homeward', 0),
-    ('depart', 3),
-    ('depart', 5),
-    ('weights', 0, 4, True, False),
-    ('depart', 4),
+    ('depart', 1),
+    ('weights', 4, 4, False, True, 1),
+    ('weights', 4, 4, False, True, 2),
     ('depart', 0),
     ('fin',),
-    ('weights', 4, 4, False, True),
 )
 
 
@@ -429,10 +433,12 @@
         def _():
             over.wait_send()
 
-    def weights(first, count, start, last):
+    def weights(first, count, start, last, only=None):
         n = count * PLANE
         r = pl.ds(first * PLANE, n)
         for a, out in enumerate((gwd_h, gwg_h, gwu_h)):
+            if only is not None and a != only:
+                continue
             for j in range(2):
                 pair = jnp.concatenate([hid[a, 2 * j, r, :], hid[a, 2 * j + 1, r, :]], axis=1)
                 v = lax.dot_general(pair, tc[1 if a == 0 else 0, r, :], FF, preferred_element_type=F32)
@@ -477,7 +483,7 @@
 
     @pl.when(home)
     def _():
-        gt_out[...] = fin[pl.ds(pl.multiple_of(k * SHARD, 8), SHARD), :].astype(BF)
+        gt_out[...] = fin[pl.ds(pl.multiple_of(k * SHARD, 8), SHARD), :]
         near.wait_send()
         for s in dz_:
             dz_[s].wait_send()
@@ -485,7 +491,7 @@
     @pl.when(jnp.logical_not(home))
     def _():
         near.wait_recv()
-        gt_out[...] = frecv[...].astype(BF)
+        gt_out[...] = frecv[...]
 
     for copy in pending:
         copy.wait_send()
@@ -493,16 +499,23 @@
         store.wait()
 
 
-def hand_over(g_in, a_in, b_in, c_in, g_out, a_out, b_out, c_out, a, b, c, into, out):
-    stays = ((a_in, a, a_out), (b_in, b, b_out), (c_in, c, c_out))
-    first = [pltpu.make_async_copy(src, via, into.at[i]) for i, (src, via, _) in enumerate(stays)]
-    second = [pltpu.make_async_copy(via, dst, out.at[i]) for i, (_, via, dst) in enumerate(stays)]
+def hand_over(g_in, a_in, b_in, c_in, g_out, a_out, b_out, c_out, g, a, b, c, into, out, g_sem):
+    first, second = [], []
+    get = pltpu.make_async_copy(g_in, g, g_sem)
+    for i, (src, via, dst) in enumerate(((c_in, c, c_out), (a_in, a, a_out), (b_in, b, b_out))):
+        n = src.shape[0] // 2
+        for j in range(2):
+            part = pl.ds(j * n, n)
+            first.append(pltpu.make_async_copy(src.at[part, :], via.at[part, :], into.at[i, j]))
+            second.append(pltpu.make_async_copy(via.at[part, :], dst.at[part, :], out.at[i, j]))
+    get.start()
     for copy in first:
         copy.start()
-    g_out[...] = g_in[...]
     for before, after in zip(first, second):
         before.wait()
         after.start()
+    get.wait()
+    g_out[...] = g[...].astype(BF)
     for copy in second:
         copy.wait()
 
@@ -514,7 +527,7 @@
     shapes = [jax.ShapeDtypeStruct(s, BF) for s in ((SHARD, WIDE), (WIDE, 512), (WIDE, 512), (512, WIDE))]
     grads = pl.pallas_call(
         kernel,
-        out_shape=shapes,
+        out_shape=[jax.ShapeDtypeStruct((SHARD, WIDE), F32)] + shapes[1:],
         in_specs=[vm, vm, hbm, hbm, hbm],
         out_specs=[vm, hbm, hbm, hbm],
         scratch_shapes=[
@@ -550,9 +563,12 @@
     return pl.pallas_call(
         hand_over,
         out_shape=shapes,
-        in_specs=[vm, hbm, hbm, hbm],
+        in_specs=[hbm] * 4,
         out_specs=[vm, hbm, hbm, hbm],
-        scratch_shapes=[V(s.shape, BF) for s in shapes[1:]] + [pltpu.SemaphoreType.DMA((3,))] * 2,
+        scratch_shapes=[V((SHARD, WIDE), F32)]
+        + [V(s.shape, BF) for s in shapes[1:]]
+        + [pltpu.SemaphoreType.DMA((3, 2))] * 2
+        + [pltpu.SemaphoreType.DMA],
         name="hand_over",
     )(*grads)
 

time: 113 us -> 109 us (0.965)
  Pallas kernels: 112 us -> 108 us
    pallas_call x2, Pallas kernels: 112 us -> 108 us  [the longest x1 104 us: local(): pl.pallas_call(kernel, out_shape=[jax.ShapeDtypeStruct((SHARD, WIDE), F32...]
where the time goes in v3:
time: 109 us; the launch traced here: 108 us
  Pallas kernels  108 us (99%)
    pallas_call x1, Pallas kernels, local(): pl.pallas_call(kernel, out_shape=[jax.ShapeDtypeStruct((SHARD, WIDE), F32...  104 us
    pallas_call x1, Pallas kernels, local(): pl.pallas_call(hand_over, out_shape=shapes, in_specs=[hbm] * 4, out_specs...  3.29 us

profile of v3, /device:TPU:1, one launch (start us, length us, event | category | flops | bytes accessed | tf_op | source)
XLA Modules:
  0.0 108.4 jit_solution(567011307632640022)
XLA Ops:
  0.6 104.4 %ffn_backward.1 = (f32[40,896]{1,0:T(8,128)}, bf16[896,512]{1,0:T(8,128)(2,1)}, bf16[896,512]{1,0:T(8,128)(2,1)}, bf16[512,896]{1,0:T(8,128)(2,1)}) custom-call(bf16[40,896]{1,0:T(8,128)(2,1)} %tok.1, bf16[40,896]{1,0:T(8,128)(2,1)} %cot.1, bf16[896,512]{1,0:T(8,128)(2,1)} %wg_h.1, bf16[896,512]{1,0:T(8,128)(2,1)} %wu_h.1, bf16[512,896]{1,0:T(8,128)(2,1)} %wd_h.1), custom_call_target="tpu_custom_call" | custom-call | tf_op jit(solution)/shard_map/ffn_backward/pallas_call | solution.py:528
  105.0 3.3 %hand_over.1 = (bf16[40,896]{1,0:T(8,128)(2,1)}, bf16[896,512]{1,0:T(8,128)(2,1)}, bf16[896,512]{1,0:T(8,128)(2,1)}, bf16[512,896]{1,0:T(8,128)(2,1)}) custom-call(f32[40,896]{1,0:T(8,128)} %get-tuple-element.8.g_in, bf16[896,512]{1,0:T(8,128)(2,1)} %get-tuple-element.9.a_in, bf16[896,512]{1,0:T(8,128)(2,1)} %get-tuple-element.10.b_in, ...), custom_call_target="tpu_custom_call" | custom-call | tf_op jit(solution)/shard_map/hand_over/pallas_call | solution.py:563

commit v4 on v3

--- a/solution.py
+++ b/solution.py
@@ -158,7 +158,6 @@
     ('weights', 4, 4, False, True, 1),
     ('weights', 4, 4, False, True, 2),
     ('depart', 0),
-    ('fin',),
 )
 
 
@@ -206,13 +205,13 @@
     barrier = pltpu.get_barrier_semaphore()
     for p in partners:
         pl.semaphore_signal(barrier, inc=1, device_id=p, device_id_type=MESH)
+    mine = jnp.where(k == 0, tok[...].astype(F32), cot[...].astype(F32))
+    xs[...] = jnp.where(k == 0, cot[...].astype(F32), tok[...].astype(F32))
     pl.semaphore_wait(barrier, len(partners))
 
     def rows(s, start, size):
         return pl.ds(pl.multiple_of(POS[s] * PLANE + start, 16), size)
 
-    mine = jnp.where(k == 0, tok[...].astype(F32), cot[...].astype(F32))
-    xs[...] = jnp.where(k == 0, cot[...].astype(F32), tok[...].astype(F32))
     first = send(xs, xr, at(dk=1))
     first.wait_recv()
     other = xr[...]
@@ -385,6 +384,17 @@
             cr[s, a].wait_recv()
         if PATHS[s]:
             gy[s].wait_recv()
+        if s == 0:
+            for h in (1 - k, k):
+                half = rows(s, h * HALF, HALF)
+                v = lax.dot_general(wide(1, half), wg[...], LL, preferred_element_type=F32)
+                v = v + lax.dot_general(wide(2, half), wu[...], LL, preferred_element_type=F32)
+                if s in dc:
+                    dpart[i, pl.ds(pl.multiple_of(k * HALF, 8), HALF), :] = v
+                else:
+                    dsend[i] = v
+                    dc[s] = send(dsend.at[i], drecv.at[i], at(dk=1))
+            return
         v = lax.dot_general(wide(1, r), wg[...], LL, preferred_element_type=F32)
         v = v + lax.dot_general(wide(2, r), wu[...], LL, preferred_element_type=F32)
         dpart[i] = v
@@ -421,11 +431,18 @@
 
         @pl.when(home)
         def _():
+            if s == 0:
+                total = dpart[i, 0:HALF, :]
+                for d in dz_:
+                    dz_[d].wait_recv()
+                    total = total + zhome[POS[d]].astype(F32)
+                zsum[...] = total
             over.wait_recv()
-            v = dpart[i, 0:HALF, :] + zrecv[i].astype(F32)
             if s == 0:
-                zsum[...] = v
+                fin[...] = zsum[...] + zrecv[i].astype(F32)
+                near.start()
             else:
+                v = dpart[i, 0:HALF, :] + zrecv[i].astype(F32)
                 zsend[i] = v.astype(BF)
                 go.start()
 
@@ -462,21 +479,11 @@
         send_sem=ss.at[NSEM], recv_sem=rs.at[NSEM], device_id=at(dk=1), device_id_type=MESH,
     )
 
-    def fin_send():
-        @pl.when(home)
-        def _():
-            total = zsum[...]
-            for s in dz_:
-                dz_[s].wait_recv()
-                total = total + zhome[POS[s]].astype(F32)
-            fin[...] = total
-            near.start()
-
     stores = []
     table = dict(
         start2=start2,
         arrive=arrive, partial=partial, relay=relay, cross=cross, finish=finish, spreadA=spreadA, spreadB=spreadB,
-        onward=onward, onwardY=onwardY, down=down, homeward=homeward, depart=depart, weights=weights, fin=fin_send,
+        onward=onward, onwardY=onwardY, down=down, homeward=homeward, depart=depart, weights=weights,
     )
     for name, *where in PROGRAM:
         table[name](*where)

time: 109 us -> 109 us (level)
  no operation moved by 1% of the time
where the time goes in v4:
time: 109 us; the launch traced here: 108 us
  Pallas kernels  108 us (99%)
    pallas_call x1, Pallas kernels, local(): pl.pallas_call(kernel, out_shape=[jax.ShapeDtypeStruct((SHARD, WIDE), F32...  104 us
    pallas_call x1, Pallas kernels, local(): pl.pallas_call(hand_over, out_shape=shapes, in_specs=[hbm] * 4, out_specs...  3.29 us

profile of v4, /device:TPU:1, one launch (start us, length us, event | category | flops | bytes accessed | tf_op | source)
XLA Modules:
  0.0 108.4 jit_solution(1363254003157040159)
XLA Ops:
  0.6 104.3 %ffn_backward.1 = (f32[40,896]{1,0:T(8,128)}, bf16[896,512]{1,0:T(8,128)(2,1)}, bf16[896,512]{1,0:T(8,128)(2,1)}, bf16[512,896]{1,0:T(8,128)(2,1)}) custom-call(bf16[40,896]{1,0:T(8,128)(2,1)} %tok.1, bf16[40,896]{1,0:T(8,128)(2,1)} %cot.1, bf16[896,512]{1,0:T(8,128)(2,1)} %wg_h.1, bf16[896,512]{1,0:T(8,128)(2,1)} %wu_h.1, bf16[512,896]{1,0:T(8,128)(2,1)} %wd_h.1), custom_call_target="tpu_custom_call" | custom-call | tf_op jit(solution)/shard_map/ffn_backward/pallas_call | solution.py:535
  104.9 3.3 %hand_over.1 = (bf16[40,896]{1,0:T(8,128)(2,1)}, bf16[896,512]{1,0:T(8,128)(2,1)}, bf16[896,512]{1,0:T(8,128)(2,1)}, bf16[512,896]{1,0:T(8,128)(2,1)}) custom-call(f32[40,896]{1,0:T(8,128)} %get-tuple-element.8.g_in, bf16[896,512]{1,0:T(8,128)(2,1)} %get-tuple-element.9.a_in, bf16[896,512]{1,0:T(8,128)(2,1)} %get-tuple-element.10.b_in, ...), custom_call_target="tpu_custom_call" | custom-call | tf_op jit(solution)/shard_map/hand_over/pallas_call | solution.py:570
